TPU v7x, 32 devices: a whole 2x2x4 slice. The times are simulated.
32 devices in a mesh: dp: 4 (over y, x), expert: 4 (over z), tensor: 2 (over core).
Axes of the slice: x: 2, y: 2, z: 4, core: 2. Of those that a mesh axis runs over, the one named last changes fastest.
Arguments:
- tokens: bfloat16 [1024, 6144], P(('dp', 'expert'), 'tensor'), may hold values from -6 to 6
- routes: int32 [1024, 2], P(('dp', 'expert')), may hold values from 0 to 3, all different within a row; in each aligned block of 64 rows (0 to 63, 64 to 127, ...) at most 34 rows name the same one
- route_weights: float32 [1024, 2], P(('dp', 'expert')), may hold values from 0.2 to 1
- gate_proj: bfloat16 [4, 6144, 8192], P('expert', 'dp', 'tensor'), may hold values from -0.078125 to 0.078125
- up_proj: bfloat16 [4, 6144, 8192], P('expert', 'dp', 'tensor'), may hold values from -0.078125 to 0.078125
- down_proj: bfloat16 [4, 8192, 6144], P('expert', 'tensor', 'dp'), may hold values from -0.0625 to 0.0625
Outputs:
- mixed: bfloat16 [1024, 6144], P(('dp', 'expert'), 'tensor')
Inputs may be any that keep to these rules, and one draw needn't show every extreme that they name: `routes`: in each aligned block of 64 rows, no expert is named by more than 34 rows, a bound that some block reaches; a row names 2 different experts.
All inputs are finite; a program needn't handle non-finite values.
Results may differ from a plain program's by a relative error of at most 0.0066.
Values may be sent and summed in bfloat16 or wider, within the bound.
A program may use at most 256 MiB of HBM per device.

v0:
```python
import jax
import jax.numpy as jnp
from jax import lax
from jax.sharding import PartitionSpec as P

TOPK = 2


def shards(tokens, routes, route_weights, gate_proj, up_proj, down_proj):
    n_tokens = tokens.shape[0]
    n_experts = lax.axis_size("expert") * gate_proj.shape[0]
    capacity = min(n_tokens, n_tokens * TOPK // n_experts + 2)
    n_slots = n_experts * capacity
    flat_routes = routes.reshape(-1)
    one_hot = (flat_routes[:, None] == jnp.arange(n_experts, dtype=jnp.int32)[None, :]).astype(
        jnp.int32
    )
    earlier = jnp.cumsum(one_hot, axis=0) - one_hot
    slot_index = jnp.sum(earlier * one_hot, axis=1)
    dest_slot = flat_routes * capacity + slot_index
    pair_owner = jnp.arange(n_tokens * TOPK, dtype=jnp.int32) // TOPK
    owners = jnp.zeros((n_slots,), jnp.int32).at[dest_slot].set(pair_owner)
    filled = (
        jnp.zeros((n_slots,), jnp.bfloat16)
        .at[dest_slot]
        .set(jnp.ones((n_tokens * TOPK,), jnp.bfloat16))
    )
    outgoing = jnp.take(tokens, owners, axis=0) * filled[:, None]
    received = lax.all_to_all(
        outgoing.reshape(n_experts, capacity, -1), "expert", split_axis=0, concat_axis=0, tiled=True
    )
    whole_rows = lax.all_gather(received.reshape(n_slots, -1), "tensor", axis=1, tiled=True)
    width_blocks = lax.all_to_all(whole_rows, "dp", split_axis=1, concat_axis=0, tiled=True)
    gate_part = jnp.dot(width_blocks, gate_proj[0], preferred_element_type=jnp.float32)
    up_part = jnp.dot(width_blocks, up_proj[0], preferred_element_type=jnp.float32)
    gate_sum, up_sum = (
        lax.psum_scatter(gate_part, "dp", scatter_dimension=0, tiled=True),
        lax.psum_scatter(up_part, "dp", scatter_dimension=0, tiled=True),
    )
    hidden = (jax.nn.silu(gate_sum) * up_sum).astype(jnp.bfloat16)
    terms = jnp.dot(
        hidden,
        lax.all_gather(down_proj[0], "dp", axis=1, tiled=True),
        preferred_element_type=jnp.float32,
    )
    expert_rows = lax.psum_scatter(
        terms.astype(jnp.bfloat16), "tensor", scatter_dimension=1, tiled=True
    )
    returned_rows = lax.all_to_all(
        expert_rows.reshape(n_experts, capacity, -1),
        "expert",
        split_axis=0,
        concat_axis=0,
        tiled=True,
    )
    returned_rows = returned_rows.reshape(n_slots, -1)
    picked = (
        jnp.take(returned_rows, dest_slot, axis=0).astype(jnp.float32).reshape(n_tokens, TOPK, -1)
    )
    mixed = jnp.sum(picked * route_weights[:, :, None], axis=1)
    return mixed.astype(jnp.bfloat16)


def solution(mesh):
    placed = (
        P(("dp", "expert"), "tensor"),
        P(("dp", "expert"), None),
        P(("dp", "expert"), None),
        P("expert", "dp", "tensor"),
        P("expert", "dp", "tensor"),
        P("expert", "tensor", "dp"),
    )
    return jax.shard_map(
        shards, mesh=mesh, in_specs=placed, out_specs=P(("dp", "expert"), "tensor"), check_vma=False
    )
```

profile of v0, /device:TPU:0, one launch (start us, length us, event | category | flops | bytes accessed | tf_op | source)
XLA Modules:
  0.0 790.6 jit_solution(1579004308773659221)
XLA Ops:
  6.5 0.8 copy.18
  7.4 0.7 broadcast_multiply_fusion
  8.0 0.1 reshape.77
  8.3 0.2 reduce_window_sum.11
  8.4 0.2 select_reduce_fusion
  8.7 0.1 mul.51
  8.9 1.0 scatter_custom_fusion
  9.9 1.1 gather_fusion
  11.0 0.2 gather.13
  11.3 1.3 scatter_custom_fusion.1
  12.8 0.2 select_multiply_fusion
  13.0 30.4 %all_to_all.29 = bf16[4,34,3072]{2,1,0:T(8,128)(2,1)S(1)} all-to-all(bf16[4,34,3072]{2,1,0:T(8,128)(2,1)S(1)} %select_multiply_fusion), channel_id=1, replica_groups=mesh['dp'=4,'expert'=4,'tensor'=2] {'expert'}, dimensions={0} | all-to-all | bytes 1671168 | tf_op jit(solution)/shard_map/all_to_all | solution.py:29
  43.4 1.1 reshape.78
  44.6 9.2 %all-gather.4.cloned.1.call-done = bf16[136,6144]{1,0:T(8,128)(2,1)} async-done(((bf16[136,3072]{1,0:T(8,128)(2,1)}), bf16[136,6144]{1,0:T(8,128)(2,1)}) %all-gather.4.cloned.1.call-update) | async-done | bytes 1671184 | tf_op jit(solution)/shard_map/all_gather | solution.py:32
  53.8 1.6 copy.26
  55.3 25.1 %all_to_all.30 = bf16[136,4,1536]{2,0,1:T(8,128)(2,1)S(1)} all-to-all(bf16[136,4,1536]{2,0,1:T(8,128)(2,1)S(1)} %bitcast.27), channel_id=1, replica_groups=mesh['dp'=4,'expert'=4,'tensor'=2] {'dp'}, dimensions={1} | all-to-all | bytes 3342336 | tf_op jit(solution)/shard_map/all_to_all | solution.py:33
  80.4 12.1 %fusion.4 = f32[544,4096]{1,0:T(8,128)} fusion(bf16[544,1536]{1,0:T(8,128)(2,1)S(1)} %bitcast.28, bf16[1,1536,4096]{2,1,0:T(8,128)(2,1)} %param.9), kind=kOutput, calls=%fused_computation.8 | convolution fusion | flops 6845104128 | bytes 23166976 | tf_op jit(solution)/shard_map/dot_general | solution.py:34
  92.6 12.1 %fusion.2 = f32[544,4096]{1,0:T(8,128)} fusion(bf16[544,1536]{1,0:T(8,128)(2,1)S(1)} %bitcast.29, bf16[1,1536,4096]{2,1,0:T(8,128)(2,1)} %param.10), kind=kOutput, calls=%fused_computation.6 | convolution fusion | flops 6845104128 | bytes 23166976 | tf_op jit(solution)/shard_map/dot_general | solution.py:35
  104.8 0.5 all-gather.6.cloned.1.call-update
  105.3 77.4 %reduce-scatter.10.cloned.1.call-done = f32[136,4096]{1,0:T(8,128)} async-done(((f32[544,4096]{1,0:T(8,128)}), f32[136,4096]{1,0:T(8,128)}) %reduce-scatter.10.cloned.1.call-update) | async-done | bytes 2228240
  182.7 93.9 %reduce-scatter.12.cloned.1.call-done = f32[136,4096]{1,0:T(8,128)} async-done(((f32[544,4096]{1,0:T(8,128)}), f32[136,4096]{1,0:T(8,128)}) %reduce-scatter.12.cloned.1.call-update) | async-done | bytes 2228240
  276.6 440.0 %all-gather.6.cloned.1.call-done = bf16[1,4096,6144]{2,1,0:T(8,128)(2,1)} async-done(((bf16[1,4096,1536]{2,1,0:T(8,128)(2,1)}), bf16[1,4096,6144]{2,1,0:T(8,128)(2,1)}) %all-gather.6.cloned.1.call-update) | async-done | bytes 50331664 | tf_op jit(solution)/shard_map/all_gather | solution.py:43
  716.6 20.7 %fusion.6 = bf16[136,6144]{1,0:T(8,128)(2,1)} fusion(bf16[1,4096,6144]{2,1,0:T(8,128)(2,1)} %all-gather.6.cloned.1.call-done, f32[136,4096]{1,0:T(8,128)} %reduce-scatter.12.cloned.1.call-done, f32[136,4096]{1,0:T(8,128)} %reduce-scatter.10.cloned.1.call-done), kind=kOutput, calls=%fused_computation.10 | convolution fusion | flops 6849282048 | bytes 56459264 | tf_op jit(solution)/shard_map/dot_general | solution.py:41
  737.4 9.3 %reduce-scatter.8.cloned.1.call-done = bf16[136,3072]{1,0:T(8,128)(2,1)} async-done(((bf16[136,6144]{1,0:T(8,128)(2,1)}), bf16[136,3072]{1,0:T(8,128)(2,1)}) %reduce-scatter.8.cloned.1.call-update) | async-done | bytes 835600 | tf_op jit(solution)/shard_map/reduce_scatter | solution.py:46
  746.7 2.3 reshape.79
  749.0 4.9 all-to-all-start.2
  753.9 0.1 reduce_sum.23
  754.4 24.3 %all-to-all-done.2 = bf16[4,34,3072]{2,1,0:T(8,128)(2,1)S(1)} async-done(((bf16[4,34,3072]{2,1,0:T(8,128)(2,1)}), bf16[4,34,3072]{2,1,0:T(8,128)(2,1)S(1)}, u32[]{:S(2)}, u32[]{:S(2)}) %all-to-all-start.2) | async-done | bytes 835616 | tf_op jit(solution)/shard_map/all_to_all | solution.py:49
  778.7 0.2 reshape.80
  778.9 1.0 gather_fusion.1
  780.0 0.3 gather.15
  780.3 3.8 multiply_reduce_fusion
  (32 shorter events, 0.9 us)
Async XLA Ops:
  6.5 3.4 copy-start
  6.5 47.2 %all-gather.4.cloned.1.call-start = ((), (), s32[]{:S(2)}) async-start(), calls=%async_computation.6 | async-start | bytes 2506752 | tf_op jit(solution)/shard_map/all_gather | solution.py:32
  44.6 138.2 %reduce-scatter.10.cloned.1.call-start = ((), (), s32[]{:S(2)}) async-start(), calls=%async_computation.9 | async-start | bytes 11141120
  92.5 184.1 %reduce-scatter.12.cloned.1.call-start = ((), (), s32[]{:S(2)}) async-start(), calls=%async_computation.10 | async-start | bytes 11141120
  104.7 611.9 %all-gather.6.cloned.1.call-start = ((), (), s32[]{:S(2)}) async-start(), calls=%async_computation.8 | async-start | bytes 62914560 | tf_op jit(solution)/shard_map/all_gather | solution.py:43
  105.3 641.4 %reduce-scatter.8.cloned.1.call-start = ((), (), s32[]{:S(2)}) async-start(), calls=%async_computation.7 | async-start | bytes 2506752 | tf_op jit(solution)/shard_map/reduce_scatter | solution.py:46
  737.4 16.7 %copy-start.2 = (s32[64,2]{0,1:T(2,128)S(1)}, s32[64,2]{0,1:T(2,128)}, u32[]{:S(2)}) copy-start(s32[64,2]{0,1:T(2,128)} %param.7) | copy-start | bytes 1540
  737.4 16.9 %copy-start.3 = (f32[64,2]{0,1:T(2,128)S(1)}, f32[64,2]{0,1:T(2,128)}, u32[]{:S(2)}) copy-start(f32[64,2]{0,1:T(2,128)} %param.8) | copy-start | bytes 1540
  749.0 29.7 %all-to-all-start.2 = ((bf16[4,34,3072]{2,1,0:T(8,128)(2,1)}), bf16[4,34,3072]{2,1,0:T(8,128)(2,1)S(1)}, u32[]{:S(2)}, u32[]{:S(2)}) async-start(bf16[4,34,3072]{2,1,0:T(8,128)(2,1)} %reshape.79), calls=%async_computation.3 | async-start | bytes 1966080 | tf_op jit(solution)/shard_map/all_to_all | solution.py:49
  778.9 5.2 copy-start.1
Sparse Core Ops, SparseCore 0:
  44.7 9.0 all-gather.3
  92.6 90.0 reduce-scatter.9
  185.9 90.7 reduce-scatter.11
  278.4 438.2 all-gather.5
  737.5 9.1 reduce-scatter.7
where the time goes:
time: 791 us
  waiting for transfers between devices  655 us (83%)
  blocking collectives  55.5 us (7%)
  matrix products  44.9 us (6%)
  between operations  13.3 us (2%)
  local copies, waits for them, and re-layouts  12 us (2%)
    all_gather x1, waiting for transfers between devices, shards(): lax.all_gather(down_proj[0], 'dp', axis=1, tiled=True)  440 us
    unnamed x7, waiting for transfers between devices  172 us
    all_to_all x1, blocking collectives, shards(): lax.all_to_all(outgoing.reshape(n_experts, capacity, -1), 'expert', split...  30.4 us
    all_to_all x1, blocking collectives, shards(): lax.all_to_all(whole_rows, 'dp', split_axis=1, concat_axis=0, tiled=True)  25.1 us
    all_to_all x1, waiting for transfers between devices, shards(): lax.all_to_all(expert_rows.reshape(n_experts, capacity, -1), 'expert', sp...  24.3 us
    dot_general x1, matrix products, shards(): jnp.dot(hidden, lax.all_gather(down_proj[0], 'dp', axis=1, tiled=True), p...  20.7 us
  transfers between devices with their start and end apart: 6, of which 6 were waited for; matrix products, arithmetic and copies ran while one was open for 2% of the time, Pallas kernels for 0%

commit v1 on v0

v1 whole, which is shorter than its diff:
```python
import jax
import jax.numpy as jnp
from jax import lax
from jax.sharding import PartitionSpec as P

TOPK = 2


def shards(tokens, routes, route_weights, gate_proj, up_proj, down_proj):
    n_tokens, part = tokens.shape
    n_experts = lax.axis_size("expert") * gate_proj.shape[0]
    n_dp, n_tensor = lax.axis_size("dp"), lax.axis_size("tensor")
    capacity = min(n_tokens, n_tokens * TOPK // n_experts + 2)
    n_slots = n_experts * capacity
    width = part * n_tensor // n_dp
    piece = width // n_tensor
    if n_dp % n_tensor == 0:
        spread = lax.all_to_all(
            tokens.reshape(n_tokens, n_dp // n_tensor, n_tensor, piece),
            "tensor", split_axis=2, concat_axis=1, tiled=True,
        )
        spread = spread.reshape(n_tokens, n_dp * piece)
    else:
        whole = lax.all_gather(tokens, "tensor", axis=1, tiled=True)
        whole = whole.reshape(n_tokens, n_dp, n_tensor, piece)
        spread = lax.dynamic_index_in_dim(whole, lax.axis_index("tensor"), 2, False)
        spread = spread.reshape(n_tokens, n_dp * piece)
    flat_routes = routes.reshape(-1)
    one_hot = (flat_routes[:, None] == jnp.arange(n_experts, dtype=jnp.int32)[None, :]).astype(
        jnp.int32
    )
    earlier = jnp.cumsum(one_hot, axis=0) - one_hot
    slot_index = jnp.sum(earlier * one_hot, axis=1)
    dest_slot = flat_routes * capacity + slot_index
    slots = jnp.arange(n_slots, dtype=jnp.int32)
    dest = dest_slot.reshape(n_tokens, TOPK)
    select = sum(
        (dest[:, k][None, :] == slots[:, None]).astype(jnp.bfloat16) for k in range(TOPK)
    )
    outgoing = jnp.dot(select, spread, preferred_element_type=jnp.float32).astype(jnp.bfloat16)
    received = lax.all_to_all(
        outgoing.reshape(n_experts, capacity, -1), "expert", split_axis=0, concat_axis=0, tiled=True
    )
    blocks = lax.all_to_all(
        received.reshape(n_slots, n_dp * piece), "dp", split_axis=1, concat_axis=0, tiled=True
    )
    rows = lax.all_gather(blocks, "tensor", axis=1, tiled=True)
    gate_part = jnp.dot(rows, gate_proj[0], preferred_element_type=jnp.float32)
    gate_sum = lax.psum_scatter(
        gate_part.astype(jnp.bfloat16), "dp", scatter_dimension=0, tiled=True
    ).astype(jnp.float32)
    up_part = jnp.dot(rows, up_proj[0], preferred_element_type=jnp.float32)
    up_sum = lax.psum_scatter(
        up_part.astype(jnp.bfloat16), "dp", scatter_dimension=0, tiled=True
    ).astype(jnp.float32)
    hidden = (jax.nn.silu(gate_sum) * up_sum).astype(jnp.bfloat16)
    hidden = lax.all_gather(hidden, "dp", axis=0, tiled=True)
    terms = jnp.dot(hidden, down_proj[0], preferred_element_type=jnp.float32)
    expert_rows = lax.psum_scatter(
        terms.astype(jnp.bfloat16), "tensor", scatter_dimension=1, tiled=True
    )
    back = lax.all_to_all(expert_rows, "dp", split_axis=0, concat_axis=1, tiled=True)
    returned = lax.all_to_all(
        back.reshape(n_experts, capacity, -1), "expert", split_axis=0, concat_axis=0, tiled=True
    ).reshape(n_slots, -1)
    picked = jnp.take(returned, dest_slot, axis=0).astype(jnp.float32)
    picked = picked.reshape(n_tokens, TOPK, -1)
    mixed = jnp.sum(picked * route_weights[:, :, None], axis=1).astype(jnp.bfloat16)
    if n_dp % n_tensor == 0:
        mixed = lax.all_to_all(
            mixed.reshape(n_tokens, n_tensor, n_dp // n_tensor, 1, piece),
            "tensor", split_axis=1, concat_axis=3, tiled=True,
        )
        return mixed.reshape(n_tokens, part)
    whole = lax.all_gather(mixed.reshape(n_tokens, n_dp, 1, piece), "tensor", axis=2, tiled=True)
    whole = whole.reshape(n_tokens, n_tensor, part)
    return lax.dynamic_index_in_dim(whole, lax.axis_index("tensor"), 1, False)


def solution(mesh):
    placed = (
        P(("dp", "expert"), "tensor"),
        P(("dp", "expert"), None),
        P(("dp", "expert"), None),
        P("expert", "dp", "tensor"),
        P("expert", "dp", "tensor"),
        P("expert", "tensor", "dp"),
    )
    return jax.shard_map(
        shards, mesh=mesh, in_specs=placed, out_specs=P(("dp", "expert"), "tensor"), check_vma=False
    )
```

time: 791 us -> 341 us (0.43)
  waiting for transfers between devices: 655 us -> 195 us
  blocking collectives: 55.5 us -> 66.1 us
    all_gather x2, waiting for transfers between devices: 449 us -> 62.9 us  [the longest x1 54.8 us: shards(): hidden = lax.all_gather(hidden, 'dp', axis=0, tiled=True)]
    unnamed x7, waiting for transfers between devices: 172 us -> 99.1 us
    all_to_all x1 -> x3, blocking collectives: 25.1 us -> 35.4 us  [the longest x1 16.4 us: shards(): lax.all_to_all(expert_rows, 'dp', split_axis=0, concat_axis=1, tiled=True)]
    dot_general x3 -> x4, matrix products: 44.9 us -> 39.8 us  [the longest x1 13.6 us: shards(): up_part = jnp.dot(rows, up_proj[0], preferred_element_type=jnp.float32)]
    all_to_all x1 -> x2, waiting for transfers between devices: 24.3 us -> 23.5 us  [the longest x1 22.8 us: shards(): lax.all_to_all(back.reshape(n_experts, capacity, -1), 'expert', split_axi...]
  transfers between devices with their start and end apart: 6 -> 7, of which waited for: 6 -> 7; matrix products, arithmetic and copies ran while one was open for 2% -> 4% of each run, Pallas kernels for 0% -> 0%
where the time goes in v1:
time: 341 us
  waiting for transfers between devices  195 us (57%)
  blocking collectives  66.1 us (19%)
  matrix products  39.8 us (12%)
  between operations  13.3 us (4%)
  local copies, waits for them, and re-layouts  11.3 us (3%)
  starting transfers between devices  8.58 us (3%)
  other arithmetic  6.88 us (2%)
    unnamed x7, waiting for transfers between devices  99.1 us
    all_gather x1, waiting for transfers between devices, shards(): hidden = lax.all_gather(hidden, 'dp', axis=0, tiled=True)  54.8 us
    all_to_all x1, blocking collectives, shards(): lax.all_to_all(outgoing.reshape(n_experts, capacity, -1), 'expert', split...  30.7 us
    all_to_all x1, waiting for transfers between devices, shards(): lax.all_to_all(back.reshape(n_experts, capacity, -1), 'expert', split_axi...  22.8 us
    all_to_all x1, blocking collectives, shards(): lax.all_to_all(expert_rows, 'dp', split_axis=0, concat_axis=1, tiled=True)  16.4 us
    all_to_all x1, blocking collectives, shards(): lax.all_to_all(received.reshape(n_slots, n_dp * piece), 'dp', split_axis=...  14.9 us
    dot_general x1, matrix products, shards(): up_part = jnp.dot(rows, up_proj[0], preferred_element_type=jnp.float32)  13.6 us
    dot_general x1, matrix products, shards(): gate_part = jnp.dot(rows, gate_proj[0], preferred_element_type=jnp.float32)  13.4 us
  transfers between devices with their start and end apart: 7, of which 7 were waited for; matrix products, arithmetic and copies ran while one was open for 4% of the time, Pallas kernels for 0%

profile of v1, /device:TPU:0, one launch (start us, length us, event | category | flops | bytes accessed | tf_op | source)
XLA Modules:
  0.0 340.7 jit_solution(7565288543876508404)
XLA Ops:
  6.5 1.3 reshape.93
  7.8 1.0 copy.43
  8.9 3.5 %all-to-all-start = ((bf16[64,2,2,768]{3,1,0,2:T(2,128)(2,1)}), bf16[64,2,2,768]{3,1,0,2:T(2,128)(2,1)S(1)}, u32[]{:S(2)}, u32[]{:S(2)}) async-start(bf16[64,2,2,768]{3,1,0,2:T(2,128)(2,1)} %copy.43), calls=%async_computation | async-start | bytes 786432 | tf_op jit(solution)/shard_map/all_to_all | solution.py:18
  13.4 0.6 all-to-all-done
  14.3 0.3 reshape.94
  14.6 0.4 convolution_convert_fusion
  15.2 30.7 %all_to_all.75 = bf16[4,34,3072]{2,1,0:T(8,128)(2,1)S(1)} all-to-all(bf16[4,34,3072]{2,1,0:T(8,128)(2,1)S(1)} %reshape.95), channel_id=1, replica_groups=mesh['dp'=4,'expert'=4,'tensor'=2] {'expert'}, dimensions={0} | all-to-all | bytes 1671168 | tf_op jit(solution)/shard_map/all_to_all | solution.py:41
  45.9 0.5 all_to_all.58
  46.5 14.9 %all_to_all.76 = bf16[136,4,768]{2,0,1:T(8,128)(2,1)} all-to-all(bf16[136,4,768]{2,0,1:T(8,128)(2,1)S(1)} %copy.45), channel_id=1, replica_groups=mesh['dp'=4,'expert'=4,'tensor'=2] {'dp'}, dimensions={1} | all-to-all | bytes 1671168 | tf_op jit(solution)/shard_map/all_to_all | solution.py:44
  61.4 8.1 %all-gather.3.cloned.1.call-done = bf16[544,1536]{1,0:T(8,128)(2,1)} async-done(((bf16[544,768]{1,0:T(8,128)(2,1)}), bf16[544,1536]{1,0:T(8,128)(2,1)}) %all-gather.3.cloned.1.call-update) | async-done | bytes 1671184 | tf_op jit(solution)/shard_map/all_gather | solution.py:47
  69.5 13.4 %fusion.6 = bf16[544,4096]{1,0:T(8,128)(2,1)} fusion(bf16[544,1536]{1,0:T(8,128)(2,1)} %all-gather.3.cloned.1.call-done, bf16[1,1536,4096]{2,1,0:T(8,128)(2,1)} %param.9), kind=kOutput, calls=%fused_computation.7 | convolution fusion | flops 6847332352 | bytes 18710528 | tf_op jit(solution)/shard_map/dot_general | solution.py:48
  83.0 1.4 copy-done.2
  84.4 13.6 %fusion.9 = bf16[544,4096]{1,0:T(8,128)(2,1)} fusion(bf16[544,1536]{1,0:T(8,128)(2,1)S(1)} %copy-done.2, bf16[1,1536,4096]{2,1,0:T(8,128)(2,1)} %param.10), kind=kOutput, calls=%fused_computation.8 | convolution fusion | flops 6847332352 | bytes 18710528 | tf_op jit(solution)/shard_map/dot_general | solution.py:52
  98.1 41.1 %reduce-scatter.10.cloned.1.call-done = bf16[136,4096]{1,0:T(8,128)(2,1)} async-done(((bf16[544,4096]{1,0:T(8,128)(2,1)}), bf16[136,4096]{1,0:T(8,128)(2,1)}) %reduce-scatter.10.cloned.1.call-update) | async-done | bytes 1114128
  139.2 58.0 %reduce-scatter.12.cloned.1.call-done = bf16[136,4096]{1,0:T(8,128)(2,1)} async-done(((bf16[544,4096]{1,0:T(8,128)(2,1)}), bf16[136,4096]{1,0:T(8,128)(2,1)}) %reduce-scatter.12.cloned.1.call-update) | async-done | bytes 1114128
  197.2 3.3 fusion.19
  200.7 54.8 %all-gather.5.cloned.1.call-done = bf16[544,4096]{1,0:T(8,128)(2,1)} async-done(((bf16[136,4096]{1,0:T(8,128)(2,1)}), bf16[544,4096]{1,0:T(8,128)(2,1)}) %all-gather.5.cloned.1.call-update) | async-done | bytes 4456464 | tf_op jit(solution)/shard_map/all_gather | solution.py:57
  255.5 12.3 %fusion.12 = bf16[544,1536]{1,0:T(8,128)(2,1)} fusion(bf16[544,4096]{1,0:T(8,128)(2,1)} %all-gather.5.cloned.1.call-done, bf16[1,4096,1536]{2,1,0:T(8,128)(2,1)} %param.11), kind=kOutput, calls=%fused_computation.10 | convolution fusion | flops 6845939712 | bytes 18710528 | tf_op jit(solution)/shard_map/dot_general | solution.py:58
  267.8 9.3 %reduce-scatter.8.cloned.1.call-done = bf16[544,768]{1,0:T(8,128)(2,1)} async-done(((bf16[544,1536]{1,0:T(8,128)(2,1)}), bf16[544,768]{1,0:T(8,128)(2,1)}) %reduce-scatter.8.cloned.1.call-update) | async-done | bytes 835600 | tf_op jit(solution)/shard_map/reduce_scatter | solution.py:59
  277.1 16.4 %all_to_all.77 = bf16[4,136,768]{2,1,0:T(8,128)(2,1)S(1)} all-to-all(bf16[4,136,768]{2,1,0:T(8,128)(2,1)} %bitcast.49), channel_id=1, replica_groups=mesh['dp'=4,'expert'=4,'tensor'=2] {'dp'}, dimensions={0} | all-to-all | bytes 1671168 | tf_op jit(solution)/shard_map/all_to_all | solution.py:62
  293.6 0.3 copy.46
  293.9 1.5 reshape.96
  295.4 4.7 %all-to-all-start.4 = ((bf16[4,34,3072]{2,1,0:T(8,128)(2,1)}), bf16[4,34,3072]{2,1,0:T(8,128)(2,1)S(1)}, u32[]{:S(2)}, u32[]{:S(2)}) async-start(bf16[4,34,3072]{2,1,0:T(8,128)(2,1)} %reshape.96), calls=%async_computation.5 | async-start | bytes 1966080 | tf_op jit(solution)/shard_map/all_to_all | solution.py:63
  300.6 22.8 %all-to-all-done.4 = bf16[4,34,3072]{2,1,0:T(8,128)(2,1)S(1)} async-done(((bf16[4,34,3072]{2,1,0:T(8,128)(2,1)}), bf16[4,34,3072]{2,1,0:T(8,128)(2,1)S(1)}, u32[]{:S(2)}, u32[]{:S(2)}) %all-to-all-start.4) | async-done | bytes 835616 | tf_op jit(solution)/shard_map/all_to_all | solution.py:63
  323.7 1.0 gather_fusion
  324.7 0.3 gather.7
  325.0 3.1 multiply_reduce_fusion
  328.1 0.3 convert_element_type.59
  328.4 0.3 copy.49
  328.7 4.0 %all_to_all.78 = bf16[64,2,2,1,768]{4,2,0,3,1:T(2,128)(2,1)S(1)} all-to-all(bf16[64,2,2,1,768]{4,2,0,3,1:T(2,128)(2,1)S(1)} %copy.49), channel_id=1, replica_groups=mesh['dp'=4,'expert'=4,'tensor'=2] {'tensor'}, dimensions={1} | all-to-all | bytes 786432 | tf_op jit(solution)/shard_map/all_to_all | solution.py:70
  332.7 0.4 copy.50
  333.2 1.0 reshape.98
  (35 shorter events, 2.7 us)
Async XLA Ops:
  6.5 5.9 %copy-start = (s32[64,2]{0,1:T(2,128)S(1)}, s32[64,2]{0,1:T(2,128)}, u32[]{:S(2)}) copy-start(s32[64,2]{0,1:T(2,128)} %param.7) | copy-start | bytes 1540
  8.9 5.1 %all-to-all-start = ((bf16[64,2,2,768]{3,1,0,2:T(2,128)(2,1)}), bf16[64,2,2,768]{3,1,0,2:T(2,128)(2,1)S(1)}, u32[]{:S(2)}, u32[]{:S(2)}) async-start(bf16[64,2,2,768]{3,1,0,2:T(2,128)(2,1)} %copy.43), calls=%async_computation | async-start | bytes 786432 | tf_op jit(solution)/shard_map/all_to_all | solution.py:18
  12.4 57.1 %all-gather.3.cloned.1.call-start = ((), (), s32[]{:S(2)}) async-start(), calls=%async_computation.9 | async-start | bytes 2506752 | tf_op jit(solution)/shard_map/all_gather | solution.py:47
  61.4 77.8 %reduce-scatter.10.cloned.1.call-start = ((), (), s32[]{:S(2)}) async-start(), calls=%async_computation.12 | async-start | bytes 5570560
  83.0 1.4 copy-start.2
  83.0 114.2 %reduce-scatter.12.cloned.1.call-start = ((), (), s32[]{:S(2)}) async-start(), calls=%async_computation.13 | async-start | bytes 5570560
  98.1 157.4 %all-gather.5.cloned.1.call-start = ((), (), s32[]{:S(2)}) async-start(), calls=%async_computation.10 | async-start | bytes 5570560 | tf_op jit(solution)/shard_map/all_gather | solution.py:57
  200.5 76.7 %reduce-scatter.8.cloned.1.call-start = ((), (), s32[]{:S(2)}) async-start(), calls=%async_computation.11 | async-start | bytes 2506752 | tf_op jit(solution)/shard_map/reduce_scatter | solution.py:59
  293.9 6.6 %copy-start.1 = (f32[64,2]{0,1:T(2,128)S(1)}, f32[64,2]{0,1:T(2,128)}, u32[]{:S(2)}) copy-start(f32[64,2]{0,1:T(2,128)} %param.8) | copy-start | bytes 1540
  295.4 28.0 %all-to-all-start.4 = ((bf16[4,34,3072]{2,1,0:T(8,128)(2,1)}), bf16[4,34,3072]{2,1,0:T(8,128)(2,1)S(1)}, u32[]{:S(2)}, u32[]{:S(2)}) async-start(bf16[4,34,3072]{2,1,0:T(8,128)(2,1)} %reshape.96), calls=%async_computation.5 | async-start | bytes 1966080 | tf_op jit(solution)/shard_map/all_to_all | solution.py:63
Sparse Core Ops, SparseCore 0:
  61.5 7.9 all-gather.2
  83.1 56.0 reduce-scatter.9
  142.3 54.8 reduce-scatter.11
  200.6 54.8 all-gather.4
  268.0 9.1 reduce-scatter.7

commit v2 on v1

--- a/solution.py
+++ b/solution.py
@@ -1,9 +1,226 @@
+import functools
+
 import jax
 import jax.numpy as jnp
 from jax import lax
+from jax.experimental import pallas as pl
+from jax.experimental.pallas import tpu as pltpu
 from jax.sharding import PartitionSpec as P
 
 TOPK = 2
+CHUNK = 256
+MESH = pl.DeviceIdType.MESH
+
+
+def kernel(
+    n_chunks, x_ref, wg_ref, wu_ref, wd_ref, out_ref,
+    xs, wt, wd, snd1, rcv1, snd2, rcv2, hid, keep, acc, ysnd, yrcv,
+    w_sem, wd_sem, x_sem, y_sem, s1, r1, s2, r2, hs, hr,
+):
+    me, ex, core = lax.axis_index("dp"), lax.axis_index("expert"), lax.axis_index("tensor")
+    mx, my = me % 2, me // 2
+    xn, yn, diag = my * 2 + 1 - mx, (1 - my) * 2 + mx, 3 - me
+    to_x, to_y, to_core = (xn, ex, core), (yn, ex, core), (me, ex, 1 - core)
+    half = x_ref.shape[1]
+    owned = n_chunks * CHUNK
+    owners = (diag, diag, xn, yn, yn, xn, me, me)
+
+    def weight(k, c, slot):
+        src = wg_ref if k % 2 == 0 else wu_ref
+        cols = pl.ds(pl.multiple_of(owners[k] * owned + c * CHUNK, CHUNK), CHUNK)
+        return pltpu.make_async_copy(src.at[:, cols], wt.at[slot, k], w_sem.at[slot, k])
+
+    def remote(src, dst, send, recv, to):
+        return pltpu.make_async_remote_copy(
+            src_ref=src, dst_ref=dst, send_sem=send, recv_sem=recv,
+            device_id=to, device_id_type=MESH,
+        )
+
+    def first(c, k):
+        return remote(snd1.at[c, k], rcv1.at[c, k], s1.at[c, k], r1.at[c, k],
+                      to_x if k % 2 == 0 else to_y)
+
+    def second(c, k):
+        return remote(snd2.at[c, k], rcv2.at[c, k], s2.at[c, k], r2.at[c, k],
+                      to_y if k == 0 else to_x)
+
+    def spread(c, k):
+        if k == 0:
+            return remote(hid.at[c, 0], hid.at[c, 1], hs.at[c, 0], hr.at[c, 0], to_x)
+        if k == 1:
+            return remote(hid.at[c, 0], hid.at[c, 2], hs.at[c, 1], hr.at[c, 1], to_y)
+        cols = pl.ds((k - 2) * (CHUNK // 2), CHUNK // 2)
+        return remote(hid.at[c, k - 1, :, cols], hid.at[c, 3, :, cols], hs.at[c, k],
+                      hr.at[c, k], to_y if k == 2 else to_x)
+
+    down_copy = pltpu.make_async_copy(wd_ref, wd, wd_sem)
+    for k in range(8):
+        weight(k, 0, 0).start()
+    barrier = pltpu.get_barrier_semaphore()
+    for to in (to_x, to_y, to_core):
+        pl.semaphore_signal(barrier, inc=1, device_id=to, device_id_type=MESH)
+    pl.semaphore_wait(barrier, 3)
+    x_copy = remote(x_ref, xs.at[core], x_sem.at[0], x_sem.at[1], to_core)
+    x_copy.start()
+    xs[core] = x_ref[...]
+    acc[...] = jnp.zeros_like(acc)
+    x_copy.wait()
+
+    def product(slot, k):
+        return jnp.dot(
+            xs[0], wt[slot, k, :half, :], preferred_element_type=jnp.float32
+        ) + jnp.dot(xs[1], wt[slot, k, half:, :], preferred_element_type=jnp.float32)
+
+    def step(i, carry):
+        @pl.when(i < n_chunks)
+        def _():
+            c = jnp.minimum(i, n_chunks - 1)
+            slot = c % 2
+
+            @pl.when(c + 1 < n_chunks)
+            def _():
+                for k in range(8):
+                    weight(k, c + 1, 1 - slot).start()
+
+            @pl.when(c == 0)
+            def _():
+                down_copy.start()
+
+            for k in range(4):
+                weight(k, c, slot).wait()
+                snd1[c, k] = product(slot, k).astype(jnp.bfloat16)
+                first(c, k).start()
+            for k in range(4, 8):
+                weight(k, c, slot).wait()
+                keep[slot, k - 4] = product(slot, k)
+
+        @pl.when((i >= 2) & (i < n_chunks + 2))
+        def _():
+            c = i - 2
+            for k in range(2):
+                spread(c, k).wait_recv()
+                spread(c, k + 2).start()
+
+        @pl.when((i >= 1) & (i < n_chunks + 1))
+        def _():
+            c = i - 1
+            for k in range(2):
+                first(c, k).wait_recv()
+                snd2[c, k] = (keep[c % 2, k] + rcv1[c, k].astype(jnp.float32)).astype(jnp.bfloat16)
+                second(c, k).start()
+
+        @pl.when(i >= 3)
+        def _():
+            c = i - 3
+
+            @pl.when(c == 0)
+            def _():
+                down_copy.wait()
+
+            spread(c, 2).wait_recv()
+            spread(c, 3).wait_recv()
+            for n in range(0, acc.shape[1], 512):
+                total = acc[:, n : n + 512]
+                for s, owner in enumerate((me, xn, yn, diag)):
+                    at = pl.ds(pl.multiple_of(owner * owned + c * CHUNK, CHUNK), CHUNK)
+                    total += jnp.dot(
+                        hid[c, s], wd[at, n : n + 512], preferred_element_type=jnp.float32
+                    )
+                acc[:, n : n + 512] = total
+
+        @pl.when((i >= 1) & (i < n_chunks + 1))
+        def _():
+            c = i - 1
+            first(c, 2).wait_recv()
+            first(c, 3).wait_recv()
+            second(c, 0).wait_recv()
+            second(c, 1).wait_recv()
+            gate = keep[c % 2, 2] + rcv1[c, 2].astype(jnp.float32) + rcv2[c, 0].astype(jnp.float32)
+            up = keep[c % 2, 3] + rcv1[c, 3].astype(jnp.float32) + rcv2[c, 1].astype(jnp.float32)
+            hid[c, 0] = (gate / (1.0 + jnp.exp(-gate)) * up).astype(jnp.bfloat16)
+            spread(c, 0).start()
+            spread(c, 1).start()
+
+        return carry
+
+    lax.fori_loop(0, n_chunks + 3, step, 0)
+    ysnd[0] = acc[:, :half].astype(jnp.bfloat16)
+    ysnd[1] = acc[:, half:].astype(jnp.bfloat16)
+    y_copy = remote(ysnd.at[1 - core], yrcv, y_sem.at[0], y_sem.at[1], to_core)
+    y_copy.start()
+
+    def drain(c, carry):
+        for k in range(4):
+            first(c, k).wait_send()
+            spread(c, k).wait_send()
+        for k in range(2):
+            second(c, k).wait_send()
+        return carry
+
+    lax.fori_loop(0, n_chunks, drain, 0)
+    y_copy.wait()
+    out_ref[...] = (ysnd[core].astype(jnp.float32) + yrcv[...].astype(jnp.float32)).astype(
+        jnp.bfloat16
+    )
+
+
+def experts(blocks, gate_proj, up_proj, down_proj):
+    rows, half = blocks.shape
+    width, ff = gate_proj.shape
+    n_chunks = ff // (4 * CHUNK)
+    vmem = pl.BlockSpec(memory_space=pltpu.VMEM)
+    hbm = pl.BlockSpec(memory_space=pl.ANY)
+    bf, dma = jnp.bfloat16, pltpu.SemaphoreType.DMA
+    return pl.pallas_call(
+        functools.partial(kernel, n_chunks),
+        out_shape=jax.ShapeDtypeStruct((rows, half), bf),
+        in_specs=[vmem, hbm, hbm, hbm],
+        out_specs=vmem,
+        scratch_shapes=[
+            pltpu.VMEM((2, rows, half), bf),
+            pltpu.VMEM((2, 8, width, CHUNK), bf),
+            pltpu.VMEM((ff, width), bf),
+            pltpu.VMEM((n_chunks, 4, rows, CHUNK), bf),
+            pltpu.VMEM((n_chunks, 4, rows, CHUNK), bf),
+            pltpu.VMEM((n_chunks, 2, rows, CHUNK), bf),
+            pltpu.VMEM((n_chunks, 2, rows, CHUNK), bf),
+            pltpu.VMEM((n_chunks, 4, rows, CHUNK), bf),
+            pltpu.VMEM((2, 4, rows, CHUNK), jnp.float32),
+            pltpu.VMEM((rows, width), jnp.float32),
+            pltpu.VMEM((2, rows, half), bf),
+            pltpu.VMEM((rows, half), bf),
+            dma((2, 8)), dma, dma((2,)), dma((2,)),
+            dma((n_chunks, 4)), dma((n_chunks, 4)),
+            dma((n_chunks, 2)), dma((n_chunks, 2)),
+            dma((n_chunks, 4)), dma((n_chunks, 4)),
+        ],
+        compiler_params=pltpu.CompilerParams(
+            collective_id=0, has_side_effects=True, vmem_limit_bytes=63 * 1024 * 1024
+        ),
+        cost_estimate=pl.CostEstimate(
+            flops=6 * rows * width * ff, bytes_accessed=6 * width * ff,
+            transcendentals=rows * ff // 4,
+        ),
+    )(blocks, gate_proj, up_proj, down_proj)
+
+
+def plain_experts(blocks, gate_proj, up_proj, down_proj):
+    rows = lax.all_gather(blocks, "tensor", axis=1, tiled=True)
+    gate_part = jnp.dot(rows, gate_proj[0], preferred_element_type=jnp.float32)
+    gate_sum = lax.psum_scatter(
+        gate_part, "dp", scatter_dimension=0, tiled=True
+    ).astype(jnp.float32)
+    up_part = jnp.dot(rows, up_proj[0], preferred_element_type=jnp.float32)
+    up_sum = lax.psum_scatter(
+        up_part, "dp", scatter_dimension=0, tiled=True
+    ).astype(jnp.float32)
+    hidden = (jax.nn.silu(gate_sum) * up_sum).astype(jnp.bfloat16)
+    hidden = lax.all_gather(hidden, "dp", axis=0, tiled=True)
+    terms = jnp.dot(hidden, down_proj[0], preferred_element_type=jnp.float32)
+    expert_rows = lax.psum_scatter(
+        terms.astype(jnp.bfloat16), "tensor", scatter_dimension=1, tiled=True
+    )
+    return expert_rows
 
 
 def shards(tokens, routes, route_weights, gate_proj, up_proj, down_proj):
@@ -44,21 +261,10 @@
     blocks = lax.all_to_all(
         received.reshape(n_slots, n_dp * piece), "dp", split_axis=1, concat_axis=0, tiled=True
     )
-    rows = lax.all_gather(blocks, "tensor", axis=1, tiled=True)
-    gate_part = jnp.dot(rows, gate_proj[0], preferred_element_type=jnp.float32)
-    gate_sum = lax.psum_scatter(
-        gate_part.astype(jnp.bfloat16), "dp", scatter_dimension=0, tiled=True
-    ).astype(jnp.float32)
-    up_part = jnp.dot(rows, up_proj[0], preferred_element_type=jnp.float32)
-    up_sum = lax.psum_scatter(
-        up_part.astype(jnp.bfloat16), "dp", scatter_dimension=0, tiled=True
-    ).astype(jnp.float32)
-    hidden = (jax.nn.silu(gate_sum) * up_sum).astype(jnp.bfloat16)
-    hidden = lax.all_gather(hidden, "dp", axis=0, tiled=True)
-    terms = jnp.dot(hidden, down_proj[0], preferred_element_type=jnp.float32)
-    expert_rows = lax.psum_scatter(
-        terms.astype(jnp.bfloat16), "tensor", scatter_dimension=1, tiled=True
-    )
+    if n_dp == 4 and n_tensor == 2 and gate_proj.shape[2] % (4 * CHUNK) == 0:
+        expert_rows = experts(blocks, gate_proj[0], up_proj[0], down_proj[0])
+    else:
+        expert_rows = plain_experts(blocks, gate_proj, up_proj, down_proj)
     back = lax.all_to_all(expert_rows, "dp", split_axis=0, concat_axis=1, tiled=True)
     returned = lax.all_to_all(
         back.reshape(n_experts, capacity, -1), "expert", split_axis=0, concat_axis=0, tiled=True

time: 341 us -> 240 us (0.70)
  waiting for transfers between devices: 195 us -> 24.2 us
  Pallas kernels: 0 us -> 128 us
  matrix products: 39.8 us -> 0.36 us
  between operations: 13.3 us -> 0.18 us
    pallas_call x0 -> x1, Pallas kernels: none -> 128 us  [experts(): pl.pallas_call(functools.partial(kernel, n_chunks), out_shape=jax.ShapeDt...]
    unnamed x7 -> x0, waiting for transfers between devices: 99.1 us -> none
    all_gather x2 -> x0, waiting for transfers between devices: 62.9 us -> none  [the longest x1 54.8 us: shards(): hidden = lax.all_gather(hidden, 'dp', axis=0, tiled=True)]
    dot_general x3 -> x0, matrix products: 39.4 us -> none  [the longest x1 13.6 us: shards(): up_part = jnp.dot(rows, up_proj[0], preferred_element_type=jnp.float32)]
    reduce_scatter x1 -> x0, waiting for transfers between devices: 9.28 us -> none  [shards(): lax.psum_scatter(terms.astype(jnp.bfloat16), 'tensor', scatter_dimension=...]
  transfers between devices with their start and end apart: 7 -> 2, of which waited for: 7 -> 2; matrix products, arithmetic and copies ran while one was open for 4% -> 1% of each run, Pallas kernels for 0% -> 0%
where the time goes in v2:
time: 240 us
  Pallas kernels  128 us (53%)
  blocking collectives  66 us (28%)
  waiting for transfers between devices  24.2 us (10%)
  local copies, waits for them, and re-layouts  9.94 us (4%)
  starting transfers between devices  7.16 us (3%)
  other arithmetic  3.54 us (1%)
    pallas_call x1, Pallas kernels, experts(): pl.pallas_call(functools.partial(kernel, n_chunks), out_shape=jax.ShapeDt...  128 us
    all_to_all x1, blocking collectives, shards(): lax.all_to_all(outgoing.reshape(n_experts, capacity, -1), 'expert', split...  30.7 us
    all_to_all x1, waiting for transfers between devices, shards(): lax.all_to_all(back.reshape(n_experts, capacity, -1), 'expert', split_axi...  23.5 us
    all_to_all x1, blocking collectives, shards(): lax.all_to_all(expert_rows, 'dp', split_axis=0, concat_axis=1, tiled=True)  16.4 us
    all_to_all x1, blocking collectives, shards(): lax.all_to_all(received.reshape(n_slots, n_dp * piece), 'dp', split_axis=...  14.9 us
  transfers between devices with their start and end apart: 2, of which 2 were waited for; matrix products, arithmetic and copies ran while one was open for 1% of the time, Pallas kernels for 0%

profile of v2, /device:TPU:0, one launch (start us, length us, event | category | flops | bytes accessed | tf_op | source)
XLA Modules:
  0.0 239.7 jit_solution(18375567443903052993)
XLA Ops:
  0.0 1.3 reshape.93
  1.3 1.0 copy.43
  2.4 3.5 %all-to-all-start = ((bf16[64,2,2,768]{3,1,0,2:T(2,128)(2,1)}), bf16[64,2,2,768]{3,1,0,2:T(2,128)(2,1)S(1)}, u32[]{:S(2)}, u32[]{:S(2)}) async-start(bf16[64,2,2,768]{3,1,0,2:T(2,128)(2,1)} %copy.43), calls=%async_computation | async-start | bytes 786432 | tf_op jit(solution)/shard_map/all_to_all | solution.py:235
  5.9 0.1 reshape.92
  6.2 0.2 reduce_window_sum.11
  6.3 0.2 select_reduce_fusion
  6.5 0.1 reduce_sum.23
  6.8 0.7 all-to-all-done
  7.5 0.3 copy.44
  7.7 0.3 reshape.94
  8.0 0.4 convolution_convert_fusion
  8.4 0.2 reshape.95
  8.6 30.7 %all_to_all.75 = bf16[4,34,3072]{2,1,0:T(8,128)(2,1)S(1)} all-to-all(bf16[4,34,3072]{2,1,0:T(8,128)(2,1)S(1)} %reshape.95), channel_id=1, replica_groups=mesh['dp'=4,'expert'=4,'tensor'=2] {'expert'}, dimensions={0} | all-to-all | bytes 1671168 | tf_op jit(solution)/shard_map/all_to_all | solution.py:258
  39.4 0.5 all_to_all.58
  39.9 14.9 %all_to_all.76 = bf16[136,4,768]{2,0,1:T(8,128)(2,1)} all-to-all(bf16[136,4,768]{2,0,1:T(8,128)(2,1)S(1)} %copy.45), channel_id=1, replica_groups=mesh['dp'=4,'expert'=4,'tensor'=2] {'dp'}, dimensions={1} | all-to-all | bytes 1671168 | tf_op jit(solution)/shard_map/all_to_all | solution.py:261
  54.8 128.3 %shard_map.64 = bf16[544,768]{1,0:T(8,128)(2,1)} custom-call(bf16[544,768]{1,0:T(8,128)(2,1)} %bitcast.32, bf16[1536,4096]{1,0:T(8,128)(2,1)} %bitcast.34, bf16[1536,4096]{1,0:T(8,128)(2,1)} %bitcast.35, bf16[4096,1536]{1,0:T(8,128)(2,1)} %bitcast.36), custom_call_target="tpu_custom_call" | custom-call | flops 20535312384 | bytes 37748736 | tf_op jit(solution)/shard_map/pallas_call | solution.py:174
  183.1 16.4 %all_to_all.77 = bf16[4,136,768]{2,1,0:T(8,128)(2,1)S(1)} all-to-all(bf16[4,136,768]{2,1,0:T(8,128)(2,1)} %bitcast.33), channel_id=1, replica_groups=mesh['dp'=4,'expert'=4,'tensor'=2] {'dp'}, dimensions={0} | all-to-all | bytes 1671168 | tf_op jit(solution)/shard_map/all_to_all | solution.py:268
  199.5 0.3 copy.46
  199.8 1.5 reshape.96
  201.3 3.7 %all-to-all-start.4 = ((bf16[4,34,3072]{2,1,0:T(8,128)(2,1)}), bf16[4,34,3072]{2,1,0:T(8,128)(2,1)S(1)}, u32[]{:S(2)}, u32[]{:S(2)}) async-start(bf16[4,34,3072]{2,1,0:T(8,128)(2,1)} %reshape.96), calls=%async_computation.4 | async-start | bytes 1966080 | tf_op jit(solution)/shard_map/all_to_all | solution.py:269
  205.1 0.1 mul.34
  205.2 0.1 copy.42
  205.5 23.5 %all-to-all-done.4 = bf16[4,34,3072]{2,1,0:T(8,128)(2,1)S(1)} async-done(((bf16[4,34,3072]{2,1,0:T(8,128)(2,1)}), bf16[4,34,3072]{2,1,0:T(8,128)(2,1)S(1)}, u32[]{:S(2)}, u32[]{:S(2)}) %all-to-all-start.4) | async-done | bytes 835616 | tf_op jit(solution)/shard_map/all_to_all | solution.py:269
  229.0 0.2 reshape.97
  229.2 1.0 gather_fusion
  230.3 0.3 gather.7
  230.6 3.1 %multiply_reduce_fusion = bf16[64,3072]{1,0:T(8,128)(2,1)S(1)} fusion(bf16[64,2,3072]{2,1,0:T(2,128)(2,1)S(1)} %gather.7, pred[64,2]{1,0:T(8,128)(4,1)S(1)} %copy.42, f32[64,2]{1,0:T(8,128)S(1)} %copy.48), kind=kLoop, calls=%fused_computation.2 | loop fusion | flops 1376256 | bytes 1180288 | tf_op jit(solution)/shard_map/reduce_sum | solution.py:274
  233.7 0.3 convert_element_type.35
  234.0 0.3 copy.49
  234.2 4.0 %all_to_all.78 = bf16[64,2,2,1,768]{4,2,0,3,1:T(2,128)(2,1)S(1)} all-to-all(bf16[64,2,2,1,768]{4,2,0,3,1:T(2,128)(2,1)S(1)} %copy.49), channel_id=1, replica_groups=mesh['dp'=4,'expert'=4,'tensor'=2] {'tensor'}, dimensions={1} | all-to-all | bytes 786432 | tf_op jit(solution)/shard_map/all_to_all | solution.py:276
  238.3 0.4 copy.50
  238.7 1.0 reshape.98
  (15 shorter events, 0.6 us)
Async XLA Ops:
  0.0 5.8 %copy-start = (s32[64,2]{0,1:T(2,128)S(1)}, s32[64,2]{0,1:T(2,128)}, u32[]{:S(2)}) copy-start(s32[64,2]{0,1:T(2,128)} %param.7) | copy-start | bytes 1540
  2.4 5.1 %all-to-all-start = ((bf16[64,2,2,768]{3,1,0,2:T(2,128)(2,1)}), bf16[64,2,2,768]{3,1,0,2:T(2,128)(2,1)S(1)}, u32[]{:S(2)}, u32[]{:S(2)}) async-start(bf16[64,2,2,768]{3,1,0,2:T(2,128)(2,1)} %copy.43), calls=%async_computation | async-start | bytes 786432 | tf_op jit(solution)/shard_map/all_to_all | solution.py:235
  199.8 5.5 %copy-start.1 = (f32[64,2]{0,1:T(2,128)S(1)}, f32[64,2]{0,1:T(2,128)}, u32[]{:S(2)}) copy-start(f32[64,2]{0,1:T(2,128)} %param.8) | copy-start | bytes 1540
  201.3 27.7 %all-to-all-start.4 = ((bf16[4,34,3072]{2,1,0:T(8,128)(2,1)}), bf16[4,34,3072]{2,1,0:T(8,128)(2,1)S(1)}, u32[]{:S(2)}, u32[]{:S(2)}) async-start(bf16[4,34,3072]{2,1,0:T(8,128)(2,1)} %reshape.96), calls=%async_computation.4 | async-start | bytes 1966080 | tf_op jit(solution)/shard_map/all_to_all | solution.py:269

commit v3 on v2

--- a/solution.py
+++ b/solution.py
@@ -92,26 +92,39 @@
                 first(c, k).start()
             for k in range(4, 8):
                 weight(k, c, slot).wait()
-                keep[slot, k - 4] = product(slot, k)
-
-        @pl.when((i >= 2) & (i < n_chunks + 2))
-        def _():
-            c = i - 2
+                keep[c % 3, k - 4] = product(slot, k)
+
+        @pl.when((i >= 1) & (i < n_chunks + 1))
+        def _():
+            c = i - 1
+            for k in range(2):
+                first(c, k).wait_recv()
+                snd2[c, k] = (keep[c % 3, k] + rcv1[c, k].astype(jnp.float32)).astype(jnp.bfloat16)
+                second(c, k).start()
+
+        @pl.when((i >= 3) & (i < n_chunks + 3))
+        def _():
+            c = i - 3
             for k in range(2):
                 spread(c, k).wait_recv()
                 spread(c, k + 2).start()
 
-        @pl.when((i >= 1) & (i < n_chunks + 1))
-        def _():
-            c = i - 1
-            for k in range(2):
-                first(c, k).wait_recv()
-                snd2[c, k] = (keep[c % 2, k] + rcv1[c, k].astype(jnp.float32)).astype(jnp.bfloat16)
-                second(c, k).start()
-
-        @pl.when(i >= 3)
-        def _():
-            c = i - 3
+        @pl.when((i >= 2) & (i < n_chunks + 2))
+        def _():
+            c = i - 2
+            first(c, 2).wait_recv()
+            first(c, 3).wait_recv()
+            second(c, 0).wait_recv()
+            second(c, 1).wait_recv()
+            gate = keep[c % 3, 2] + rcv1[c, 2].astype(jnp.float32) + rcv2[c, 0].astype(jnp.float32)
+            up = keep[c % 3, 3] + rcv1[c, 3].astype(jnp.float32) + rcv2[c, 1].astype(jnp.float32)
+            hid[c, 0] = (gate / (1.0 + jnp.exp(-gate)) * up).astype(jnp.bfloat16)
+            spread(c, 0).start()
+            spread(c, 1).start()
+
+        @pl.when(i >= 4)
+        def _():
+            c = i - 4
 
             @pl.when(c == 0)
             def _():
@@ -128,22 +141,9 @@
                     )
                 acc[:, n : n + 512] = total
 
-        @pl.when((i >= 1) & (i < n_chunks + 1))
-        def _():
-            c = i - 1
-            first(c, 2).wait_recv()
-            first(c, 3).wait_recv()
-            second(c, 0).wait_recv()
-            second(c, 1).wait_recv()
-            gate = keep[c % 2, 2] + rcv1[c, 2].astype(jnp.float32) + rcv2[c, 0].astype(jnp.float32)
-            up = keep[c % 2, 3] + rcv1[c, 3].astype(jnp.float32) + rcv2[c, 1].astype(jnp.float32)
-            hid[c, 0] = (gate / (1.0 + jnp.exp(-gate)) * up).astype(jnp.bfloat16)
-            spread(c, 0).start()
-            spread(c, 1).start()
-
         return carry
 
-    lax.fori_loop(0, n_chunks + 3, step, 0)
+    lax.fori_loop(0, n_chunks + 4, step, 0)
     ysnd[0] = acc[:, :half].astype(jnp.bfloat16)
     ysnd[1] = acc[:, half:].astype(jnp.bfloat16)
     y_copy = remote(ysnd.at[1 - core], yrcv, y_sem.at[0], y_sem.at[1], to_core)
@@ -185,7 +185,7 @@
             pltpu.VMEM((n_chunks, 2, rows, CHUNK), bf),
             pltpu.VMEM((n_chunks, 2, rows, CHUNK), bf),
             pltpu.VMEM((n_chunks, 4, rows, CHUNK), bf),
-            pltpu.VMEM((2, 4, rows, CHUNK), jnp.float32),
+            pltpu.VMEM((3, 4, rows, CHUNK), jnp.float32),
             pltpu.VMEM((rows, width), jnp.float32),
             pltpu.VMEM((2, rows, half), bf),
             pltpu.VMEM((rows, half), bf),
@@ -255,20 +255,22 @@
         (dest[:, k][None, :] == slots[:, None]).astype(jnp.bfloat16) for k in range(TOPK)
     )
     outgoing = jnp.dot(select, spread, preferred_element_type=jnp.float32).astype(jnp.bfloat16)
-    received = lax.all_to_all(
-        outgoing.reshape(n_experts, capacity, -1), "expert", split_axis=0, concat_axis=0, tiled=True
-    )
-    blocks = lax.all_to_all(
-        received.reshape(n_slots, n_dp * piece), "dp", split_axis=1, concat_axis=0, tiled=True
-    )
+    planes = ("dp", "expert")
+    n_groups, lanes = n_dp * n_experts, 128 if piece % 128 == 0 else piece
+    outgoing = outgoing.reshape(n_experts, capacity, n_dp, piece // lanes, lanes)
+    outgoing = outgoing.transpose(2, 0, 3, 1, 4).reshape(n_groups, -1, lanes)
+    received = lax.all_to_all(outgoing, planes, split_axis=0, concat_axis=0, tiled=True)
+    received = received.reshape(n_groups, piece // lanes, capacity, lanes)
+    blocks = received.transpose(0, 2, 1, 3).reshape(n_groups * capacity, piece)
     if n_dp == 4 and n_tensor == 2 and gate_proj.shape[2] % (4 * CHUNK) == 0:
         expert_rows = experts(blocks, gate_proj[0], up_proj[0], down_proj[0])
     else:
         expert_rows = plain_experts(blocks, gate_proj, up_proj, down_proj)
-    back = lax.all_to_all(expert_rows, "dp", split_axis=0, concat_axis=1, tiled=True)
-    returned = lax.all_to_all(
-        back.reshape(n_experts, capacity, -1), "expert", split_axis=0, concat_axis=0, tiled=True
-    ).reshape(n_slots, -1)
+    leaving = expert_rows.reshape(n_groups, capacity, piece // lanes, lanes)
+    leaving = leaving.transpose(0, 2, 1, 3).reshape(n_groups, -1, lanes)
+    returned = lax.all_to_all(leaving, planes, split_axis=0, concat_axis=0, tiled=True)
+    returned = returned.reshape(n_dp, n_experts, piece // lanes, capacity, lanes)
+    returned = returned.transpose(1, 3, 0, 2, 4).reshape(n_slots, -1)
     picked = jnp.take(returned, dest_slot, axis=0).astype(jnp.float32)
     picked = picked.reshape(n_tokens, TOPK, -1)
     mixed = jnp.sum(picked * route_weights[:, :, None], axis=1).astype(jnp.bfloat16)

time: 240 us -> 212 us (0.88)
  blocking collectives: 66 us -> 35.7 us
  local copies, waits for them, and re-layouts: 9.94 us -> 15.5 us
  Pallas kernels: 128 us -> 125 us
    all_to_all x3 -> x1, blocking collectives: 62 us -> 31.6 us  [shards(): lax.all_to_all(outgoing, planes, split_axis=0, concat_axis=0, tiled=True)]
    pallas_call x1, Pallas kernels: 128 us -> 125 us  [experts(): pl.pallas_call(functools.partial(kernel, n_chunks), out_shape=jax.ShapeDt...]
    reshape x3 -> x5, local copies, waits for them, and re-layouts: 1.95 us -> 5.28 us  [the longest x1 2.03 us: shards(): leaving = expert_rows.reshape(n_groups, capacity, piece // lanes, lanes)]
where the time goes in v3:
time: 212 us; the launch traced here: 211 us
  Pallas kernels  125 us (59%)
  blocking collectives  35.7 us (17%)
  waiting for transfers between devices  24 us (11%)
  local copies, waits for them, and re-layouts  15.5 us (7%)
  starting transfers between devices  7.31 us (3%)
  other arithmetic  3.54 us (2%)
    pallas_call x1, Pallas kernels, experts(): pl.pallas_call(functools.partial(kernel, n_chunks), out_shape=jax.ShapeDt...  125 us
    all_to_all x1, blocking collectives, shards(): lax.all_to_all(outgoing, planes, split_axis=0, concat_axis=0, tiled=True)  31.6 us
    all_to_all x1, waiting for transfers between devices, shards(): lax.all_to_all(leaving, planes, split_axis=0, concat_axis=0, tiled=True)  23.3 us
  transfers between devices with their start and end apart: 2, of which 2 were waited for; matrix products, arithmetic and copies ran while one was open for 1% of the time, Pallas kernels for 0%

profile of v3, /device:TPU:0, one launch (start us, length us, event | category | flops | bytes accessed | tf_op | source)
XLA Modules:
  0.0 211.2 jit_solution(11792769539069592863)
XLA Ops:
  0.0 1.3 reshape.99
  1.3 1.0 copy.59
  2.4 3.5 %all-to-all-start = ((bf16[64,2,2,768]{3,1,0,2:T(2,128)(2,1)}), bf16[64,2,2,768]{3,1,0,2:T(2,128)(2,1)S(1)}, u32[]{:S(2)}, u32[]{:S(2)}) async-start(bf16[64,2,2,768]{3,1,0,2:T(2,128)(2,1)} %copy.59), calls=%async_computation | async-start | bytes 786432 | tf_op jit(solution)/shard_map/all_to_all | solution.py:235
  6.2 0.2 reduce_window_sum.11
  6.8 0.7 all-to-all-done
  7.5 0.3 copy.60
  7.7 0.3 reshape.100
  8.0 0.4 convolution_convert_fusion
  8.4 1.0 reshape.101
  9.4 0.6 copy.61
  10.1 0.2 copy.62
  10.3 31.6 %all_to_all.40 = bf16[16,204,128]{2,1,0:T(8,128)(2,1)S(1)} all-to-all(bf16[16,204,128]{2,1,0:T(8,128)(2,1)S(1)} %copy.62), channel_id=1, replica_groups=mesh['dp'=4,'expert'=4,'tensor'=2] {'dp','expert'}, dimensions={0} | all-to-all | bytes 1671168 | tf_op jit(solution)/shard_map/all_to_all | solution.py:262
  41.9 0.2 copy.63
  42.1 0.4 copy.64
  42.5 1.0 copy.75
  43.5 124.6 %shard_map.64 = bf16[544,768]{1,0:T(8,128)(2,1)} custom-call(bf16[544,768]{1,0:T(8,128)(2,1)} %bitcast.48, bf16[1536,4096]{1,0:T(8,128)(2,1)} %bitcast.49, bf16[1536,4096]{1,0:T(8,128)(2,1)} %bitcast.50, bf16[4096,1536]{1,0:T(8,128)(2,1)} %bitcast.51), custom_call_target="tpu_custom_call" | custom-call | flops 20535312384 | bytes 37748736 | tf_op jit(solution)/shard_map/pallas_call | solution.py:174
  168.2 2.0 reshape.105
  170.2 0.2 copy.65
  170.5 1.1 copy.66
  171.6 3.8 %all-to-all-start.2 = ((bf16[16,204,128]{2,1,0:T(8,128)(2,1)}), bf16[16,204,128]{2,1,0:T(8,128)(2,1)S(1)}, u32[]{:S(2)}, u32[]{:S(2)}) async-start(bf16[16,204,128]{2,1,0:T(8,128)(2,1)} %copy.66), calls=%async_computation.2 | async-start | bytes 1703936 | tf_op jit(solution)/shard_map/all_to_all | solution.py:271
  175.9 23.3 %all-to-all-done.2 = bf16[16,204,128]{2,1,0:T(8,128)(2,1)S(1)} async-done(((bf16[16,204,128]{2,1,0:T(8,128)(2,1)}), bf16[16,204,128]{2,1,0:T(8,128)(2,1)S(1)}, u32[]{:S(2)}, u32[]{:S(2)}) %all-to-all-start.2) | async-done | bytes 835616 | tf_op jit(solution)/shard_map/all_to_all | solution.py:271
  199.3 0.2 copy.67
  199.5 0.4 copy.68
  199.8 0.9 reshape.108
  200.7 1.0 gather_fusion
  201.8 0.3 gather.7
  202.1 3.1 %multiply_reduce_fusion = bf16[64,3072]{1,0:T(8,128)(2,1)S(1)} fusion(bf16[64,2,3072]{2,1,0:T(2,128)(2,1)S(1)} %gather.7, pred[64,2]{1,0:T(8,128)(4,1)S(1)} %copy.58, f32[64,2]{1,0:T(8,128)S(1)} %copy.70), kind=kLoop, calls=%fused_computation.2 | loop fusion | flops 1376256 | bytes 1180288 | tf_op jit(solution)/shard_map/reduce_sum | solution.py:276
  205.2 0.3 convert_element_type.35
  205.5 0.3 copy.71
  205.7 4.0 %all_to_all.41 = bf16[64,2,2,1,768]{4,2,0,3,1:T(2,128)(2,1)S(1)} all-to-all(bf16[64,2,2,1,768]{4,2,0,3,1:T(2,128)(2,1)S(1)} %copy.71), channel_id=1, replica_groups=mesh['dp'=4,'expert'=4,'tensor'=2] {'tensor'}, dimensions={1} | all-to-all | bytes 786432 | tf_op jit(solution)/shard_map/all_to_all | solution.py:278
  209.8 0.4 copy.72
  210.2 1.0 reshape.109
  (19 shorter events, 1.2 us)
Async XLA Ops:
  0.0 5.8 %copy-start = (s32[64,2]{0,1:T(2,128)S(1)}, s32[64,2]{0,1:T(2,128)}, u32[]{:S(2)}) copy-start(s32[64,2]{0,1:T(2,128)} %param.7) | copy-start | bytes 1540
  2.4 5.1 %all-to-all-start = ((bf16[64,2,2,768]{3,1,0,2:T(2,128)(2,1)}), bf16[64,2,2,768]{3,1,0,2:T(2,128)(2,1)S(1)}, u32[]{:S(2)}, u32[]{:S(2)}) async-start(bf16[64,2,2,768]{3,1,0,2:T(2,128)(2,1)} %copy.59), calls=%async_computation | async-start | bytes 786432 | tf_op jit(solution)/shard_map/all_to_all | solution.py:235
  170.4 5.4 %copy-start.1 = (f32[64,2]{0,1:T(2,128)S(1)}, f32[64,2]{0,1:T(2,128)}, u32[]{:S(2)}) copy-start(f32[64,2]{0,1:T(2,128)} %param.8) | copy-start | bytes 1540
  171.6 27.7 %all-to-all-start.2 = ((bf16[16,204,128]{2,1,0:T(8,128)(2,1)}), bf16[16,204,128]{2,1,0:T(8,128)(2,1)S(1)}, u32[]{:S(2)}, u32[]{:S(2)}) async-start(bf16[16,204,128]{2,1,0:T(8,128)(2,1)} %copy.66), calls=%async_computation.2 | async-start | bytes 1703936 | tf_op jit(solution)/shard_map/all_to_all | solution.py:271
